TPU v7x, 32 devices: a whole 2x2x4 slice. The times are simulated.
32 devices in a mesh: ctx: 16 (over z, y, x), pipe: 2 (over core).
Axes of the slice: x: 2, y: 2, z: 4, core: 2. Of those that a mesh axis runs over, the one named last changes fastest.
Arguments:
- activations: float32 [2, 1, 2048, 4096], P('pipe', None, 'ctx'), may hold values from -6 to 6
- norm_gain: bfloat16 [2, 8, 4096], P('pipe', None, 'ctx'), may hold values from 0.5 to 2, as said below
- w_query: bfloat16 [2, 8, 4096, 512], P('pipe', None, 'ctx'), may hold values from -0.09375 to 0.09375
- w_keyval: bfloat16 [2, 8, 4096, 256], P('pipe', None, 'ctx'), may hold values from -0.09375 to 0.09375
- w_out: bfloat16 [2, 8, 512, 4096], P('pipe', None, None, 'ctx'), may hold values from -0.25 to 0.25
- segment_ids: int32 [1, 2048], replicated, may hold values from 0 to 3, as said below
- layer_order: int32 [2, 2], P(None, 'pipe'), may hold values from 0 to 7
Outputs:
- final_stream: float32 [2, 1, 2048, 4096], P('pipe', None, 'ctx')
Inputs may be any that keep to these rules, and one draw needn't show every extreme that they name: `segment_ids`: each row never falls; every document holds 1 to 1024 positions and the last one holds exactly 1024. `norm_gain`: positive.
All inputs are finite; a program needn't handle non-finite values.
Results may differ from a plain program's by a relative error of at most 0.015.
Values may be sent and summed in bfloat16 or wider, within the bound.
A program may use at most 128 MiB of HBM per device.

v0:
```python
import functools
import itertools
import math

import jax
import jax.numpy as jnp
from jax import lax
from jax.experimental import pallas as pl
from jax.experimental.pallas import tpu as pltpu
from jax.sharding import PartitionSpec as P

TICKS = 2


def passed_along(array, axis, by):
    length = lax.axis_size(axis)
    return lax.ppermute(array, axis, [(i, (i + by) % length) for i in range(length)])


def grid_of(count):
    known = {16: (4, 2, 2), 32: (4, 8)}
    return known.get(count, (count,))


def orders_of(sizes):
    dims = tuple(range(len(sizes)))
    if len(dims) == 1:
        return (dims, dims)
    return (dims, dims[:-2] + (dims[-1], dims[-2]))


def layers_kernel(sizes, cuts, *refs):
    weights = 2 * TICKS
    count = len(cuts)
    stream, bias = refs[0], refs[1]
    out = refs[2 + weights]
    scratch = refs[3 + weights :]
    blocks = refs[2 : 2 + weights] + scratch[:TICKS]
    wholes = scratch[TICKS : TICKS + count]
    queries, attended, leaving, arriving = scratch[TICKS + count : TICKS + count + 4]
    send_sems, recv_sems, own_sems, pipe_sems = scratch[TICKS + count + 4 :]
    rank = len(sizes)
    strides = [math.prod(sizes[d + 1 :]) for d in range(rank)]
    ctx_count = math.prod(sizes)
    me = lax.axis_index("ctx")
    coords = [(me // strides[d]) % sizes[d] for d in range(rank)]
    pipe_count = lax.axis_size("pipe")
    section = lax.axis_index("pipe")

    def place(delta):
        return sum(((coords[d] + delta[d]) % sizes[d]) * strides[d] for d in range(rank))

    def along(dim, by):
        return tuple(by if d == dim else 0 for d in range(rank))

    def flat(delta):
        return sum(delta[d] * strides[d] for d in range(rank))

    barrier = pltpu.get_barrier_semaphore()
    greeted = 0
    for dim in range(rank):
        for by in range(1, sizes[dim]):
            pl.semaphore_signal(
                barrier,
                inc=1,
                device_id={"ctx": place(along(dim, by))},
                device_id_type=pl.DeviceIdType.MESH,
            )
            greeted += 1
    for by in sorted({1, pipe_count - 1}):
        pl.semaphore_signal(
            barrier,
            inc=1,
            device_id={"pipe": (section + by) % pipe_count},
            device_id_type=pl.DeviceIdType.MESH,
        )
        greeted += 1
    pl.semaphore_wait(barrier, greeted)

    orders = orders_of(sizes)
    started = []
    used = {}

    def copy_of(which, part, delta, dim, by, send):
        rows = pl.ds(*cuts[which][part])
        landing = wholes[which].at[place(delta), rows]
        origin = landing if any(delta) else blocks[which].at[rows]
        seen = tuple((sizes[d] - by) % sizes[d] if d == dim else delta[d] for d in range(rank))
        return pltpu.make_async_remote_copy(
            src_ref=origin,
            dst_ref=landing,
            send_sem=send_sems.at[which, part, send],
            recv_sem=recv_sems.at[which, part, flat(seen)],
            device_id={"ctx": place(along(dim, by))},
            device_id_type=pl.DeviceIdType.MESH,
        )

    def pass_on(which, part, delta, phases):
        for phase in phases:
            dim = orders[part][phase]
            for by in range(1, sizes[dim]):
                send = used.get((which, part), 0)
                used[which, part] = send + 1
                copy = copy_of(which, part, delta, dim, by, send)
                copy.start()
                started.append(copy)

    def take(which, phase):
        for part, order in enumerate(orders):
            ranges = [range(1)] * rank
            for before in order[:phase]:
                ranges[before] = range(sizes[before])
            ranges[order[phase]] = range(1, sizes[order[phase]])
            for delta in itertools.product(*ranges):
                landing = wholes[which].at[place(delta), pl.ds(*cuts[which][part])]
                pltpu.make_async_remote_copy(
                    src_ref=landing,
                    dst_ref=landing,
                    send_sem=send_sems.at[which, part, 0],
                    recv_sem=recv_sems.at[which, part, flat(delta)],
                    device_id={"ctx": place(along(order[phase], 1))},
                    device_id_type=pl.DeviceIdType.MESH,
                ).wait_recv()
                pass_on(which, part, delta, range(phase + 1, rank))

    def own_copy(which):
        return pltpu.make_async_copy(blocks[which], wholes[which].at[me], own_sems.at[which])

    def begin(which):
        own_copy(which).start()
        for part in range(len(orders)):
            pass_on(which, part, (0,) * rank, range(rank))

    tok_rows, model_width = stream.shape
    in_rows = model_width // ctx_count
    query_width = attended.shape[1]
    head_dim = queries.shape[-1]
    head_count = query_width // head_dim
    scale = 1.0 / math.sqrt(head_dim)

    def columns(index):
        return pl.ds(pl.multiple_of(index * in_rows, in_rows), in_rows)

    def project(tick, source):
        own_copy(2 * tick).wait()
        whole = wholes[2 * tick]

        def square(index, total):
            value = source[:, columns(index)].astype(jnp.float32)
            return total + jnp.sum(value * value, axis=1, keepdims=True)

        squares = lax.fori_loop(0, ctx_count, square, jnp.zeros((tok_rows, 1), jnp.float32))
        factor = lax.rsqrt(squares / model_width + 1e-05)

        def piece(index, total):
            value = source[:, columns(index)].astype(jnp.float32)
            gain = wholes[0][index, in_rows : in_rows + 16, :in_rows].astype(jnp.float32)
            gain = gain[tick : tick + 1]
            hidden = (value * factor * gain).astype(jnp.bfloat16)
            return total + jnp.dot(
                hidden, whole[index, :in_rows, :], preferred_element_type=jnp.float32
            )

        width = whole.shape[-1]
        sums = lax.fori_loop(0, ctx_count, piece, jnp.zeros((tok_rows, width), jnp.float32))
        low = sums.astype(jnp.bfloat16)
        for head in range(head_count):
            queries[head] = low[:, head * head_dim : (head + 1) * head_dim]
        blocks[weights + tick][...] = low[:, query_width:]

    def attend(tick):
        own_copy(weights + tick).wait()
        whole = wholes[weights + tick]
        keys = whole[:, :, :head_dim].reshape(ctx_count * tok_rows, head_dim)
        values = whole[:, :, head_dim:].reshape(ctx_count * tok_rows, head_dim)
        for head in range(head_count):
            scores = lax.dot_general(
                queries[head], keys, (((1,), (1,)), ((), ())), preferred_element_type=jnp.float32
            )
            scores = scores * scale + bias[...]
            probs = jnp.exp(scores - jnp.max(scores, axis=1, keepdims=True))
            totals = jnp.sum(probs, axis=1, keepdims=True)
            summed = jnp.dot(
                probs.astype(jnp.bfloat16), values, preferred_element_type=jnp.float32
            )
            attended[:, head * head_dim : (head + 1) * head_dim] = (summed / totals).astype(
                jnp.bfloat16
            )

    def mix(tick, source, target):
        own_copy(2 * tick + 1).wait()
        whole = wholes[2 * tick + 1]

        @pl.loop(0, ctx_count)
        def _(index):
            mixed = jnp.dot(attended[...], whole[index], preferred_element_type=jnp.float32)
            value = source[:, columns(index)].astype(jnp.float32) + mixed
            target[:, columns(index)] = value.astype(jnp.bfloat16)

    last = rank - 1
    begin(0)
    begin(1)
    take(0, 0)
    begin(2)
    for phase in range(1, rank):
        take(0, phase)
        take(1, phase - 1)
    project(0, stream)
    begin(4)
    begin(3)
    for phase in range(rank):
        take(4, phase)
        if phase < last:
            take(2, phase)
    attend(0)
    for phase in range(last):
        take(3, phase)
    take(1, last)
    mix(0, stream, leaving)
    onward = pltpu.make_async_remote_copy(
        src_ref=leaving,
        dst_ref=arriving,
        send_sem=pipe_sems.at[0],
        recv_sem=pipe_sems.at[1],
        device_id={"pipe": (section + 1) % pipe_count},
        device_id_type=pl.DeviceIdType.MESH,
    )
    onward.start()
    take(2, last)
    onward.wait()
    project(1, arriving)
    begin(5)
    for phase in range(rank):
        take(5, phase)
    attend(1)
    take(3, last)
    mix(1, arriving, out)
    for copy in started:
        copy.wait_send()


def run_layers(stream, bias, blocks, ctx_count, head_dim):
    tok_rows = stream.shape[0]
    query_width = blocks[1].shape[0]
    kv_width = blocks[0].shape[1] - query_width
    shapes = [block.shape for block in blocks] + [(tok_rows, kv_width)] * TICKS
    cuts = []
    for rows, _ in shapes:
        first = rows // 32 * 16
        cuts.append(((0, first), (first, rows - first)))
    count = len(shapes)
    parts = len(cuts[0])
    low = jnp.bfloat16
    vmem = pl.BlockSpec(memory_space=pltpu.VMEM)
    return pl.pallas_call(
        functools.partial(layers_kernel, grid_of(ctx_count), tuple(cuts)),
        out_shape=jax.ShapeDtypeStruct(stream.shape, low),
        in_specs=[vmem, vmem] + [pl.BlockSpec(memory_space=pl.ANY)] * len(blocks),
        out_specs=vmem,
        scratch_shapes=[pltpu.VMEM((tok_rows, kv_width), low)] * TICKS
        + [pltpu.VMEM((ctx_count, *shape), low) for shape in shapes]
        + [
            pltpu.VMEM((query_width // head_dim, tok_rows, head_dim), low),
            pltpu.VMEM((tok_rows, query_width), low),
            pltpu.VMEM(stream.shape, low),
            pltpu.VMEM(stream.shape, low),
            pltpu.SemaphoreType.DMA((count, parts, ctx_count)),
            pltpu.SemaphoreType.DMA((count, parts, ctx_count)),
            pltpu.SemaphoreType.DMA((count,)),
            pltpu.SemaphoreType.DMA((2,)),
        ],
        compiler_params=pltpu.CompilerParams(
            collective_id=0, has_side_effects=True, vmem_limit_bytes=56 * 1024 * 1024
        ),
    )(stream, bias, *blocks)


def row_positions(rows, tok_rows, ctx_count):
    half = tok_rows // 2
    block = rows // tok_rows
    offset = rows % tok_rows
    return jnp.where(
        offset < half, block * half + offset, (2 * ctx_count - 1 - block) * half + offset - half
    )


def pick(stacked, layer):
    return lax.dynamic_index_in_dim(stacked[0], layer, 0, keepdims=False)


def body(activations, norm_gain, w_query, w_keyval, w_out, segment_ids, layer_order):
    ctx_count = lax.axis_size("ctx")
    ctx_index = lax.axis_index("ctx")
    state = activations[0]
    seqs_here, tok_rows, model_width = state.shape
    query_width = w_query.shape[-1]
    kv_width = w_keyval.shape[-1]
    head_dim = kv_width // 2
    in_rows = w_query.shape[2]
    wide = query_width + kv_width
    in_parts, out_parts = [], []
    for tick in range(TICKS):
        layer = layer_order[tick, 0]
        both = jnp.concatenate([pick(w_query, layer), pick(w_keyval, layer)], axis=1)
        if tick == 0:
            gains = jnp.stack([pick(norm_gain, layer_order[t, 0]) for t in range(TICKS)])
            gains = jnp.pad(gains, ((0, 16 - TICKS), (0, wide - in_rows)))
            both = jnp.concatenate([both, gains], axis=0)
        in_parts.append(both)
        out_parts.append(pick(w_out, layer))
    query_pos = row_positions(
        ctx_index * tok_rows + lax.iota(jnp.int32, tok_rows), tok_rows, ctx_count
    )
    halves = segment_ids.reshape(seqs_here, 2, ctx_count, tok_rows // 2)
    by_row = jnp.stack([halves[:, 0], halves[:, 1, ::-1]], axis=2)
    key_seg = by_row.reshape(seqs_here, ctx_count * tok_rows)
    query_seg = lax.dynamic_slice_in_dim(key_seg, ctx_index * tok_rows, tok_rows, axis=1)
    key_pos = row_positions(lax.iota(jnp.int32, ctx_count * tok_rows), tok_rows, ctx_count)
    allowed = (key_pos[None, None, :] <= query_pos[None, :, None]) & (
        key_seg[:, None, :] == query_seg[:, :, None]
    )
    bias = jnp.where(allowed[0], 0.0, -1e30)
    blocks = [part for pair in zip(in_parts, out_parts) for part in pair]
    state = run_layers(state[0], bias, blocks, ctx_count, head_dim)
    state = passed_along(state, "pipe", 1).astype(jnp.float32)[None]
    return state[None]


def solution(mesh):
    in_specs = (
        P("pipe", None, "ctx", None),
        P("pipe", None, "ctx"),
        P("pipe", None, "ctx", None),
        P("pipe", None, "ctx", None),
        P("pipe", None, None, "ctx"),
        P(),
        P(None, "pipe"),
    )
    out_specs = P("pipe", None, "ctx", None)
    return jax.shard_map(body, mesh=mesh, in_specs=in_specs, out_specs=out_specs, check_vma=False)
```

profile of v0, /device:TPU:0, one launch (start us, length us, event | category | flops | bytes accessed | tf_op | source)
XLA Modules:
  0.0 252.9 jit_solution(10961052361624748893)
XLA Ops:
  0.0 1.3 fusion.25
  3.7 0.5 broadcast.211
  4.2 1.4 reduce.3
  5.6 0.1 reshape.133
  5.7 0.1 reshape.134
  5.8 0.1 eq.24
  7.0 0.8 fusion.21
  7.8 1.0 dynamic-slice_bitcast_fusion.4
  8.8 1.9 dynamic-slice_bitcast_fusion
  10.7 1.1 dynamic-slice_bitcast_fusion.1
  11.8 0.8 pad_maximum_fusion.1.refs_4_
  12.6 0.8 pad_maximum_fusion.refs_2_
  13.4 1.2 and_select_fusion.refs_1_
  14.6 233.9 %shard_map.73 = bf16[128,4096]{1,0:T(8,128)(2,1)} custom-call(f32[128,4096]{1,0:T(8,128)} %bitcast.28, f32[128,2048]{1,0:T(8,128)} %and_select_fusion.refs_1_, bf16[272,768]{1,0:T(8,128)(2,1)} %pad_maximum_fusion.refs_2_, bf16[512,256]{1,0:T(8,128)(2,1)} %get-tuple-element.6.refs_3_, bf16[256,768]{1,0:T(8,128)(2,1)} %pad_maximum_fusion.1.refs_4_, ...), custom_call_target="tpu_custom_call" | custom-call | tf_op jit(solution)/shard_map/pallas_call | solution.py:255
  248.4 0.1 collective-permute-start
  248.5 2.9 %collective-permute-done = bf16[128,4096]{1,0:T(8,128)(2,1)S(1)} collective-permute-done((bf16[128,4096]{1,0:T(8,128)(2,1)}, bf16[128,4096]{1,0:T(8,128)(2,1)S(1)}, u32[]{:S(2)}, u32[]{:S(2)}) %collective-permute-start) | collective-permute-done | bytes 1048608 | tf_op jit(solution)/shard_map/ppermute | solution.py:17
  251.4 1.5 bitcast_convert_fusion
  (7 shorter events, 0.1 us)
Async XLA Ops:
  248.4 2.9 %collective-permute-start = (bf16[128,4096]{1,0:T(8,128)(2,1)}, bf16[128,4096]{1,0:T(8,128)(2,1)S(1)}, u32[]{:S(2)}, u32[]{:S(2)}) collective-permute-start(bf16[128,4096]{1,0:T(8,128)(2,1)} %shard_map.73), channel_id=1, source_target_pairs={{0,1},{1,0},{2,3},{3,2},{4,5},{5,4},{6,7},{7,6},{8,9},{9,8},{10,11... | collective-permute-start | bytes 3145736 | tf_op jit(solution)/shard_map/ppermute | solution.py:17
where the time goes:
time: 253 us
  Pallas kernels  234 us (92%)
  local copies, waits for them, and re-layouts  6.79 us (3%)
  other arithmetic  5.71 us (2%)
  between operations  3.6 us (1%)
  waiting for transfers between devices  2.86 us (1%)
    pallas_call x1, Pallas kernels, run_layers(): pl.pallas_call(functools.partial(layers_kernel, grid_of(ctx_count), tuple...  234 us
  transfers between devices with their start and end apart: 1, of which 1 were waited for; matrix products, arithmetic and copies ran while one was open for 0% of the time, Pallas kernels for 0%

commit v1 on v0

v1 whole, which is shorter than its diff:
```python
import functools
import itertools
import math

import jax
import jax.numpy as jnp
from jax import lax
from jax.experimental import pallas as pl
from jax.experimental.pallas import tpu as pltpu
from jax.sharding import PartitionSpec as P

TICKS = 2
HALVES = 2
MESH = pl.DeviceIdType.MESH
LOW = jnp.bfloat16
FULL = jnp.float32


def grid_of(count):
    known = {
        16: ((2, 2, 2, 2), (1, 3), (0, 2), (0, 1), (2, 3)),
        32: ((4, 8), (0,), (1,), (0,), (1,)),
    }
    return known[count]


class Grid:
    def __init__(self, count):
        self.sizes, self.split_dims, self.share_dims, self.major_dims, self.minor_dims = grid_of(count)
        self.rank = len(self.sizes)
        self.strides = [math.prod(self.sizes[d + 1 :]) for d in range(self.rank)]
        self.split = self.deltas(self.split_dims)
        self.share = self.deltas(self.share_dims)
        self.major = self.deltas(self.major_dims)
        self.minor = self.deltas(self.minor_dims)
        self.hops = [
            self.along(d, by) for d in self.share_dims for by in range(1, self.sizes[d])
        ]
        self.zero = (0,) * self.rank

    def deltas(self, dims):
        ranges = [range(self.sizes[d]) if d in dims else range(1) for d in range(self.rank)]
        return list(itertools.product(*ranges))

    def along(self, dim, by):
        return tuple(by if d == dim else 0 for d in range(self.rank))

    def flat(self, delta):
        return sum(delta[d] * self.strides[d] for d in range(self.rank))

    def minus(self, one, other):
        return tuple((a - b) % s for a, b, s in zip(one, other, self.sizes))

    def plus(self, one, other):
        return tuple((a + b) % s for a, b, s in zip(one, other, self.sizes))

    def within(self, coords, dims):
        total = 0
        for d in dims:
            total = total * self.sizes[d] + coords[d]
        return total


def layers_kernel(grid, *refs):
    order, stream_hbm, gain_hbm, query_hbm, keyval_hbm, out_hbm, segments = refs[:7]
    result = refs[7]
    (
        stream,
        gains,
        query_all,
        keyval_all,
        out_all,
        sent,
        kept,
        next_kept,
        first_sum,
        w_keyval,
        w_query,
        w_out,
        later_keyval,
        later_query,
        later_out,
        part_keyval,
        part_query,
        came_keyval,
        came_query,
        part_square,
        came_square,
        keyvals,
        attended,
        back,
        came_back,
        bias,
        load_sems,
        x_send,
        x_recv,
        w_send,
        w_recv,
        pk_send,
        pk_recv,
        pq_send,
        pq_recv,
        sq_send,
        sq_recv,
        kv_send,
        kv_recv,
        at_send,
        at_recv,
        b_send,
        b_recv,
    ) = refs[8:]
    sizes = grid.sizes
    ctx_count = math.prod(sizes)
    me = lax.axis_index("ctx")
    section = lax.axis_index("pipe")
    pipe_count = lax.axis_size("pipe")
    coords = [(me // grid.strides[d]) % sizes[d] for d in range(grid.rank)]
    split_count, share_count = len(grid.split), len(grid.share)
    tok_rows, model_width = stream.shape
    half = tok_rows // HALVES
    block = model_width // ctx_count
    wide = block * share_count
    query_width = w_query.shape[-1]
    kv_width = w_keyval.shape[-1]
    head_dim = kv_width // 2
    head_count = query_width // head_dim
    scale = 1.0 / math.sqrt(head_dim)
    stacked = split_count * half

    def moved(delta):
        return [(coords[d] + delta[d]) % sizes[d] for d in range(grid.rank)]

    def place(delta):
        return sum(c * s for c, s in zip(moved(delta), grid.strides))

    def split_slot(delta):
        return grid.within(moved(delta), grid.split_dims)

    def share_slot(delta):
        return grid.within(moved(delta), grid.share_dims)

    def rank_of(half_index, delta):
        where = place(delta)
        return where if half_index == 0 else ctx_count - 1 - where

    def columns(index):
        return pl.ds(pl.multiple_of(index * block, block), block)

    def rows(half_index):
        return pl.ds(half_index * half, half)

    finish = []

    def remote(src, dst, send, recv, ctx, pipe=None):
        device = {"ctx": ctx} if pipe is None else {"ctx": ctx, "pipe": pipe}
        return pltpu.make_async_remote_copy(
            src_ref=src,
            dst_ref=dst,
            send_sem=send,
            recv_sem=recv,
            device_id=device,
            device_id_type=MESH,
        )

    def push(copy, when=None):
        if when is None:
            copy.start()
        else:
            pl.when(when)(copy.start)
        finish.append((copy, when))

    loads = []

    def load(src, dst):
        copy = pltpu.make_async_copy(src, dst, load_sems.at[len(loads)])
        copy.start()
        loads.append(copy)
        return copy

    load_stream = [load(stream_hbm.at[rows(h)], stream.at[rows(h)]) for h in range(HALVES)]
    load_gain = load(gain_hbm, gains)
    load_keyval = load(keyval_hbm, keyval_all)
    load_query = load(query_hbm, query_all)
    load_out = load(out_hbm, out_all)

    keyvals[...] = jnp.zeros_like(keyvals)

    near = sorted(
        set(grid.split + grid.hops + grid.major + grid.minor) - {grid.zero}
    )
    barrier = pltpu.get_barrier_semaphore()
    greeted = 0
    for delta in near:
        pl.semaphore_signal(
            barrier, inc=1, device_id={"ctx": place(delta)}, device_id_type=MESH
        )
        greeted += 1
    for by in sorted({1, pipe_count - 1}):
        for delta in [grid.zero] + grid.hops:
            pl.semaphore_signal(
                barrier,
                inc=1,
                device_id={"ctx": place(delta), "pipe": (section + by) % pipe_count},
                device_id_type=MESH,
            )
            greeted += 1

    key_rel = lax.broadcasted_iota(jnp.int32, (half, ctx_count * half), 1)
    row_rel = lax.broadcasted_iota(jnp.int32, (half, ctx_count * half), 0)
    for h in range(HALVES):
        query_rel = row_rel + rank_of(h, grid.zero) * half
        seg = segments[:, h * ctx_count * half : (h + 1) * ctx_count * half].astype(FULL)
        seg = jnp.broadcast_to(seg, (half, ctx_count * half))
        own = jnp.sum(jnp.where(key_rel == query_rel, seg, 0.0), axis=1, keepdims=True)
        bias[h] = jnp.where((key_rel <= query_rel) & (seg == own), 0.0, -1e30)

    pl.semaphore_wait(barrier, greeted)

    others = [delta for delta in grid.split if delta != grid.zero]
    factors = {}

    def send_stream(h):
        load_stream[h].wait()
        squares = jnp.zeros((half, 1), FULL)
        for index, delta in enumerate(grid.split):
            target = kept.at[h, split_slot(grid.zero)] if delta == grid.zero else sent.at[h, index]
            for s, share in enumerate(grid.share):
                where = grid.plus(delta, share)
                value = stream[rows(h), columns(place(where))]
                squares += jnp.sum(value * value, axis=1, keepdims=True)
                target[:, columns(share_slot(share))] = value.astype(LOW)
            if delta != grid.zero:
                seen = grid.split.index(grid.minus(grid.zero, delta))
                push(
                    remote(
                        sent.at[h, index],
                        kept.at[h, split_slot(grid.zero)],
                        x_send.at[h, index],
                        x_recv.at[h, seen],
                        place(delta),
                    )
                )
        factors[0, h] = lax.rsqrt(squares / model_width + 1e-05)

    def take_stream(h):
        for index, delta in enumerate(grid.split):
            if delta != grid.zero:
                landing = kept.at[h, split_slot(delta)]
                remote(
                    landing, landing, x_send.at[h, index], x_recv.at[h, index], place(delta)
                ).wait_recv()

    wholes = [w_keyval, w_query, w_out]
    laters = [later_keyval, later_query, later_out]
    used = {}

    def fill(kind, tick):
        layer = order[tick, 0]
        source = [keyval_all, query_all, out_all][kind]
        value = source[layer]
        if kind < 2:
            level = lax.broadcasted_iota(jnp.int32, gains.shape, 0)
            gain = jnp.where(level == layer, gains[...].astype(FULL), 0.0)
            gain = jnp.sum(gain, axis=0, keepdims=True)
            gain = jnp.transpose(jnp.broadcast_to(gain, (128, block)))
            value = value.astype(FULL)
            value = jnp.concatenate(
                [value[:, c : c + 128] * gain for c in range(0, value.shape[1], 128)], axis=1
            ).astype(LOW)
        if tick == 0:
            wholes[kind][tick, share_slot(grid.zero)] = value
        else:
            laters[kind][...] = value

    def next_send(kind, tick):
        count = used.get((kind, tick), 0)
        used[kind, tick] = count + 1
        return w_send.at[kind, tick, count]

    def begin(kind, tick):
        slot = share_slot(grid.zero)
        landing = wholes[kind].at[tick, slot]
        source = landing if tick == 0 else laters[kind]
        pipe = None if tick == 0 else (section + pipe_count - tick) % pipe_count
        for delta in grid.hops:
            seen = grid.share.index(grid.minus(grid.zero, delta))
            push(
                remote(
                    source,
                    landing,
                    next_send(kind, tick),
                    w_recv.at[kind, tick, seen],
                    place(delta),
                    pipe,
                )
            )
        if tick:
            push(
                remote(
                    source,
                    landing,
                    next_send(kind, tick),
                    w_recv.at[kind, tick, 0],
                    me,
                    pipe,
                )
            )

    def take_weight(kind, tick, phase):
        dims = grid.share_dims
        if phase == 0 and tick:
            landing = wholes[kind].at[tick, share_slot(grid.zero)]
            remote(
                landing,
                landing,
                w_send.at[kind, tick, 0],
                w_recv.at[kind, tick, 0],
                me,
                (section + pipe_count - tick) % pipe_count,
            ).wait_recv()
        for delta in grid.share:
            if delta[dims[phase]] == 0 or any(delta[d] for d in dims[phase + 1 :]):
                continue
            landing = wholes[kind].at[tick, share_slot(delta)]
            remote(
                landing,
                landing,
                w_send.at[kind, tick, 0],
                w_recv.at[kind, tick, grid.share.index(delta)],
                place(grid.along(dims[phase], 1)),
            ).wait_recv()
            for dim in dims[phase + 1 :]:
                for by in range(1, sizes[dim]):
                    hop = grid.along(dim, by)
                    seen = grid.share.index(grid.minus(delta, hop))
                    push(
                        remote(
                            landing,
                            landing,
                            next_send(kind, tick),
                            w_recv.at[kind, tick, seen],
                            place(hop),
                        )
                    )

    phases = range(len(grid.share_dims))
    layered = [kept, next_kept]

    def project(kind, tick, h):
        part = [part_keyval, part_query][kind]
        came = [came_keyval, came_query][kind]
        send, recv = [(pk_send, pk_recv), (pq_send, pq_recv)][kind]
        width = part.shape[-1]
        value = layered[tick][h].reshape(stacked, wide)
        weight = wholes[kind][tick].reshape(wide, width)
        total = jnp.dot(value, weight, preferred_element_type=FULL).astype(LOW)
        part[tick, h] = total.reshape(split_count, half, width)
        for index, delta in enumerate(grid.split):
            if delta != grid.zero:
                seen = grid.split.index(grid.minus(grid.zero, delta))
                push(
                    remote(
                        part.at[tick, h, split_slot(delta)],
                        came.at[tick, h, seen],
                        send.at[tick, h, index],
                        recv.at[tick, h, seen],
                        place(delta),
                    )
                )

    def summed(kind, tick, h):
        part = [part_keyval, part_query][kind]
        came = [came_keyval, came_query][kind]
        send, recv = [(pk_send, pk_recv), (pq_send, pq_recv)][kind]
        total = part[tick, h, split_slot(grid.zero)].astype(FULL)
        for index, delta in enumerate(grid.split):
            if delta != grid.zero:
                landing = came.at[tick, h, index]
                remote(
                    landing,
                    landing,
                    send.at[tick, h, index],
                    recv.at[tick, h, index],
                    place(delta),
                ).wait_recv()
                total += came[tick, h, index].astype(FULL)
        return (total * factors[tick, h]).astype(LOW)

    def send_squares(h, total):
        ones = jnp.ones((8, 128), FULL)
        for index, delta in enumerate(grid.split):
            piece = total[index * half : (index + 1) * half]
            piece = jnp.concatenate([piece] * (128 // half), axis=0)
            part_square[h, index] = lax.dot_general(
                ones,
                piece,
                (((1,), (1,)), ((), ())),
                preferred_element_type=FULL,
                precision=lax.Precision.HIGHEST,
            )
        for index, delta in enumerate(grid.split):
            if delta != grid.zero:
                seen = grid.split.index(grid.minus(grid.zero, delta))
                push(
                    remote(
                        part_square.at[h, split_slot(delta)],
                        came_square.at[h, seen],
                        sq_send.at[h, index],
                        sq_recv.at[h, seen],
                        place(delta),
                    )
                )

    def take_squares(h):
        total = part_square[h, split_slot(grid.zero)]
        for index, delta in enumerate(grid.split):
            if delta != grid.zero:
                landing = came_square.at[h, index]
                remote(
                    landing, landing, sq_send.at[h, index], sq_recv.at[h, index], place(delta)
                ).wait_recv()
                total += came_square[h, index]
        column = jnp.transpose(total)[:half, 0:1]
        factors[1, h] = lax.rsqrt(column / model_width + 1e-05)

    def before(h, delta):
        theirs = grid.within(moved(delta), grid.major_dims)
        ours = grid.within(coords, grid.major_dims)
        return theirs < ours if h == 0 else theirs > ours

    def after(h, delta):
        theirs = grid.within(moved(delta), grid.major_dims)
        ours = grid.within(coords, grid.major_dims)
        return theirs > ours if h == 0 else theirs < ours

    def relay(tick, h, delta, hop, when):
        landing = keyvals.at[tick, h, rank_of(h, delta)]
        seen = grid.minus(delta, hop)
        push(
            remote(
                landing,
                landing,
                kv_send.at[tick, h, grid.flat(grid.plus(delta, hop))],
                kv_recv.at[tick, h, grid.flat(seen)],
                place(hop),
            ),
            when,
        )

    def send_keyvals(tick, h):
        keyvals[tick, h, rank_of(h, grid.zero)] = summed(0, tick, h)
        for delta in grid.major:
            if delta != grid.zero:
                relay(tick, h, grid.zero, delta, after(h, delta))
        for hop in grid.minor:
            if hop != grid.zero:
                relay(tick, h, grid.zero, hop, None)

    def wait_keyvals(tick, h, delta):
        landing = keyvals.at[tick, h, rank_of(h, delta)]
        remote(
            landing,
            landing,
            kv_send.at[tick, h, 0],
            kv_recv.at[tick, h, grid.flat(delta)],
            place(grid.along(0, 1)),
        ).wait_recv()

    def pass_keyvals(tick, h):
        for delta in grid.major:
            if delta != grid.zero:
                when = before(h, delta)
                pl.when(when)(functools.partial(wait_keyvals, tick, h, delta))
                for hop in grid.minor:
                    if hop != grid.zero:
                        relay(tick, h, delta, hop, when)

    def take_keyvals(tick, h):
        for hop in grid.minor:
            if hop != grid.zero:
                wait_keyvals(tick, h, hop)
        for delta in grid.major:
            if delta != grid.zero:

                @pl.when(before(h, delta))
                def _(delta=delta):
                    for hop in grid.minor:
                        if hop != grid.zero:
                            wait_keyvals(tick, h, grid.plus(delta, hop))

    def attend(tick, h):
        query = summed(1, tick, h)
        query = jnp.concatenate(
            [query[:, i * head_dim : (i + 1) * head_dim] for i in range(head_count)], axis=0
        )
        take_keyvals(tick, h)
        keys = keyvals[tick, h, :, :, :head_dim].reshape(ctx_count * half, head_dim)
        values = keyvals[tick, h, :, :, head_dim:].reshape(ctx_count * half, head_dim)
        scores = lax.dot_general(
            query, keys, (((1,), (1,)), ((), ())), preferred_element_type=FULL
        )
        scores = scores.reshape(head_count, half, ctx_count * half) * scale + bias[h][None]
        probs = jnp.exp(scores - jnp.max(scores, axis=-1, keepdims=True))
        totals = jnp.sum(probs, axis=-1, keepdims=True)
        mixed = jnp.dot(
            probs.astype(LOW).reshape(head_count * half, ctx_count * half),
            values,
            preferred_element_type=FULL,
        ).reshape(head_count, half, head_dim)
        mixed = (mixed / totals).astype(LOW)
        own = attended.at[tick, h, split_slot(grid.zero)]
        for i in range(head_count):
            own[:, i * head_dim : (i + 1) * head_dim] = mixed[i]
        for index, delta in enumerate(grid.split):
            if delta != grid.zero:
                seen = grid.split.index(grid.minus(grid.zero, delta))
                push(
                    remote(
                        own,
                        own,
                        at_send.at[tick, h, index],
                        at_recv.at[tick, h, seen],
                        place(delta),
                    )
                )

    def take_attended(tick, h):
        for index, delta in enumerate(grid.split):
            if delta != grid.zero:
                landing = attended.at[tick, h, split_slot(delta)]
                remote(
                    landing,
                    landing,
                    at_send.at[tick, h, index],
                    at_recv.at[tick, h, index],
                    place(delta),
                ).wait_recv()

    def mix_first(h):
        take_attended(0, h)
        value = attended[0, h].reshape(stacked, query_width)
        squares = jnp.zeros((stacked, 128), FULL)
        for s in range(share_count):
            cols = pl.ds(s * block, block)
            mixed = jnp.dot(value, w_out[0, s], preferred_element_type=FULL)
            first_sum[h, :, :, cols] = mixed.reshape(split_count, half, block)
            following = kept[h, :, :, cols].reshape(stacked, block).astype(FULL) + mixed
            next_kept[h, :, :, cols] = following.astype(LOW).reshape(split_count, half, block)
            following = following * following
            for c in range(0, block, 128):
                squares += following[:, c : c + 128]
        send_squares(h, squares)

    def mix_last(h):
        take_attended(1, h)
        value = attended[1, h].reshape(stacked, query_width)
        for s in range(share_count):
            cols = pl.ds(s * block, block)
            mixed = jnp.dot(value, w_out[1, s], preferred_element_type=FULL)
            mixed = mixed.reshape(split_count, half, block) + first_sum[h, :, :, cols]
            back[h, :, :, cols] = mixed.astype(LOW)
        for index, delta in enumerate(grid.split):
            if delta != grid.zero:
                seen = grid.split.index(grid.minus(grid.zero, delta))
                push(
                    remote(
                        back.at[h, split_slot(delta)],
                        came_back.at[h, seen],
                        b_send.at[h, index],
                        b_recv.at[h, seen],
                        place(delta),
                    )
                )

    def end(h):
        for index, delta in enumerate(grid.split):
            if delta == grid.zero:
                source = back.at[h, split_slot(grid.zero)]
            else:
                source = came_back.at[h, index]
                remote(
                    source, source, b_send.at[h, index], b_recv.at[h, index], place(delta)
                ).wait_recv()
            for share in grid.share:
                cols = columns(place(grid.plus(delta, share)))
                value = source[:, columns(share_slot(share))].astype(FULL)
                result[rows(h), cols] = stream[rows(h), cols] + value

    halves = range(HALVES)
    send_stream(0)
    load_gain.wait()
    load_keyval.wait()
    fill(0, 0)
    begin(0, 0)
    send_stream(1)
    load_query.wait()
    fill(1, 0)
    begin(1, 0)
    load_out.wait()
    fill(2, 0)
    begin(2, 0)
    for kind in range(3):
        fill(kind, 1)
    for phase in phases:
        take_weight(0, 0, phase)
    for h in halves:
        take_stream(h)
        project(0, 0, h)
    for h in halves:
        send_keyvals(0, h)
    take_weight(1, 0, 0)
    for h in halves:
        pass_keyvals(0, h)
    for phase in phases[1:]:
        take_weight(1, 0, phase)
    for h in halves:
        project(1, 0, h)
    begin(0, 1)
    begin(1, 1)
    take_weight(2, 0, 0)
    for h in halves:
        attend(0, h)
    for phase in phases[1:]:
        take_weight(2, 0, phase)
    begin(2, 1)
    take_weight(0, 1, 0)
    mix_first(0)
    for phase in phases[1:]:
        take_weight(0, 1, phase)
    project(0, 1, 0)
    mix_first(1)
    project(0, 1, 1)
    for h in halves:
        take_squares(h)
        send_keyvals(1, h)
    take_weight(1, 1, 0)
    for h in halves:
        pass_keyvals(1, h)
    for phase in phases[1:]:
        take_weight(1, 1, phase)
    for h in halves:
        project(1, 1, h)
    take_weight(2, 1, 0)
    for h in halves:
        attend(1, h)
    for phase in phases[1:]:
        take_weight(2, 1, phase)
    for h in halves:
        mix_last(h)
    for h in halves:
        end(h)
    for copy, when in finish:
        if when is None:
            copy.wait_send()
        else:
            pl.when(when)(copy.wait_send)


def run_layers(order, stream, gain, query, keyval, out, segments, ctx_count):
    grid = Grid(ctx_count)
    split, share = len(grid.split), len(grid.share)
    tok_rows, model_width = stream.shape
    half = tok_rows // HALVES
    block = model_width // ctx_count
    wide = block * share
    query_width, kv_width = query.shape[-1], keyval.shape[-1]
    vmem = pl.BlockSpec(memory_space=pltpu.VMEM)
    hbm = pl.BlockSpec(memory_space=pl.ANY)
    smem = pl.BlockSpec(memory_space=pltpu.SMEM)
    dma = pltpu.SemaphoreType.DMA
    scratch = [
        pltpu.VMEM(stream.shape, FULL),
        pltpu.VMEM(gain.shape, LOW),
        pltpu.VMEM(query.shape, LOW),
        pltpu.VMEM(keyval.shape, LOW),
        pltpu.VMEM(out.shape, LOW),
        pltpu.VMEM((HALVES, split, half, wide), LOW),
        pltpu.VMEM((HALVES, split, half, wide), LOW),
        pltpu.VMEM((HALVES, split, half, wide), LOW),
        pltpu.VMEM((HALVES, split, half, wide), FULL),
        pltpu.VMEM((TICKS, share, block, kv_width), LOW),
        pltpu.VMEM((TICKS, share, block, query_width), LOW),
        pltpu.VMEM((TICKS, share, query_width, block), LOW),
        pltpu.VMEM((block, kv_width), LOW),
        pltpu.VMEM((block, query_width), LOW),
        pltpu.VMEM((query_width, block), LOW),
        pltpu.VMEM((TICKS, HALVES, split, half, kv_width), LOW),
        pltpu.VMEM((TICKS, HALVES, split, half, query_width), LOW),
        pltpu.VMEM((TICKS, HALVES, split, half, kv_width), LOW),
        pltpu.VMEM((TICKS, HALVES, split, half, query_width), LOW),
        pltpu.VMEM((HALVES, split, 8, 128), FULL),
        pltpu.VMEM((HALVES, split, 8, 128), FULL),
        pltpu.VMEM((TICKS, HALVES, ctx_count, half, kv_width), LOW),
        pltpu.VMEM((TICKS, HALVES, split, half, query_width), LOW),
        pltpu.VMEM((HALVES, split, half, wide), LOW),
        pltpu.VMEM((HALVES, split, half, wide), LOW),
        pltpu.VMEM((HALVES, half, ctx_count * half), FULL),
        dma((8,)),
        dma((HALVES, split)),
        dma((HALVES, split)),
        dma((3, TICKS, share + 2)),
        dma((3, TICKS, share)),
    ]
    scratch += [dma((TICKS, HALVES, split))] * 4
    scratch += [dma((HALVES, split))] * 2
    scratch += [dma((TICKS, HALVES, ctx_count))] * 2
    scratch += [dma((TICKS, HALVES, split))] * 2
    scratch += [dma((HALVES, split))] * 2
    return pl.pallas_call(
        functools.partial(layers_kernel, grid),
        out_shape=jax.ShapeDtypeStruct(stream.shape, FULL),
        in_specs=[smem] + [hbm] * 5 + [vmem],
        out_specs=vmem,
        scratch_shapes=scratch,
        compiler_params=pltpu.CompilerParams(
            collective_id=0, has_side_effects=True, vmem_limit_bytes=56 * 1024 * 1024
        ),
    )(order, stream, gain, query, keyval, out, segments)


def body(activations, norm_gain, w_query, w_keyval, w_out, segment_ids, layer_order):
    ctx_count = lax.axis_size("ctx")
    pipe_count = lax.axis_size("pipe")
    state = run_layers(
        layer_order,
        activations[0, 0],
        norm_gain[0],
        w_query[0],
        w_keyval[0],
        w_out[0],
        segment_ids,
        ctx_count,
    )
    if TICKS % pipe_count:
        pairs = [(i, (i + TICKS) % pipe_count) for i in range(pipe_count)]
        state = lax.ppermute(state, "pipe", pairs)
    return state[None, None]


def solution(mesh):
    in_specs = (
        P("pipe", None, "ctx", None),
        P("pipe", None, "ctx"),
        P("pipe", None, "ctx", None),
        P("pipe", None, "ctx", None),
        P("pipe", None, None, "ctx"),
        P(),
        P(None, "pipe"),
    )
    out_specs = P("pipe", None, "ctx", None)
    return jax.shard_map(body, mesh=mesh, in_specs=in_specs, out_specs=out_specs, check_vma=False)
```

time: 253 us -> 126 us (0.50)
  Pallas kernels: 234 us -> 122 us
  other arithmetic: 5.71 us -> 0 us
  between operations: 3.6 us -> 0.01 us
  waiting for transfers between devices: 2.86 us -> 0 us
    pallas_call x1, Pallas kernels: 234 us -> 122 us  [run_layers(): pl.pallas_call(functools.partial(layers_kernel, grid), out_shape=jax.Shap...]
    squeeze x3 -> x0, local copies, waits for them, and re-layouts: 3.93 us -> none  [pick(): return lax.dynamic_index_in_dim(stacked[0], layer, 0, keepdims=False)]
    unnamed x1 -> x2, local copies, waits for them, and re-layouts: 0.51 us -> 4.41 us
    ppermute x1 -> x0, waiting for transfers between devices: 2.86 us -> none  [passed_along(): lax.ppermute(array, axis, [(i, (i + by) % length) for i in range(length)])]
  transfers between devices with their start and end apart: 1 -> 0, of which waited for: 1 -> 0; matrix products, arithmetic and copies ran while one was open for 0% -> 0% of each run, Pallas kernels for 0% -> 0%
where the time goes in v1:
time: 126 us
  Pallas kernels  122 us (97%)
  local copies, waits for them, and re-layouts  4.41 us (4%)
    pallas_call x1, Pallas kernels, run_layers(): pl.pallas_call(functools.partial(layers_kernel, grid), out_shape=jax.Shap...  122 us
    unnamed x2, local copies, waits for them, and re-layouts  4.41 us

profile of v1, /device:TPU:0, one launch (start us, length us, event | category | flops | bytes accessed | tf_op | source)
XLA Modules:
  0.0 126.2 jit_solution(13946663246362009808)
XLA Ops:
  0.0 1.3 %copy.8.refs_0_ = s32[2,1]{1,0:T(2,128)} copy(s32[2,1]{0,1:T(1,128)} %param.13) | data formatting | bytes 16 | tf_op args[6]
  1.3 121.8 %shard_map.73 = f32[128,4096]{1,0:T(8,128)} custom-call(s32[2,1]{1,0:T(2,128)} %copy.8.refs_0_, f32[128,4096]{1,0:T(8,128)} %bitcast.7, bf16[8,256]{1,0:T(8,128)(2,1)} %bitcast.11, bf16[8,256,512]{2,1,0:T(8,128)(2,1)} %bitcast.8, bf16[8,256,256]{2,1,0:T(8,128)(2,1)} %bitcast.10, bf16[8,512,256]{2,1,0:T(8,128)(2,1)} %bitcast.9, s32[1,2048]{1,0:T(1,128)} %refs_6_.1), custom_call_target="tpu_custom_call" | custom-call | tf_op jit(solution)/shard_map/pallas_call | solution.py:709
  123.1 3.1 %copy.10 = f32[1,1,128,4096]{3,2,1,0:T(8,128)} copy(f32[1,1,128,4096]{3,2,1,0:T(8,128)} %bitcast.6) | data formatting | bytes 4194304

commit v2 on v1

--- a/solution.py
+++ b/solution.py
@@ -255,7 +255,7 @@
     used = {}
 
     def fill(kind, tick):
-        layer = order[tick, 0]
+        layer = order[0, tick]
         source = [keyval_all, query_all, out_all][kind]
         value = source[layer]
         if kind < 2:
@@ -594,21 +594,22 @@
     begin(0, 0)
     send_stream(1)
     load_query.wait()
+    load_out.wait()
     fill(1, 0)
-    begin(1, 0)
-    load_out.wait()
     fill(2, 0)
-    begin(2, 0)
     for kind in range(3):
         fill(kind, 1)
     for phase in phases:
         take_weight(0, 0, phase)
-    for h in halves:
-        take_stream(h)
-        project(0, 0, h)
+    take_stream(0)
+    begin(1, 0)
+    project(0, 0, 0)
+    take_stream(1)
+    project(0, 0, 1)
     for h in halves:
         send_keyvals(0, h)
     take_weight(1, 0, 0)
+    begin(2, 0)
     for h in halves:
         pass_keyvals(0, h)
     for phase in phases[1:]:
@@ -616,13 +617,12 @@
     for h in halves:
         project(1, 0, h)
     begin(0, 1)
+    take_weight(2, 0, 0)
     begin(1, 1)
-    take_weight(2, 0, 0)
     for h in halves:
         attend(0, h)
     for phase in phases[1:]:
         take_weight(2, 0, phase)
-    begin(2, 1)
     take_weight(0, 1, 0)
     mix_first(0)
     for phase in phases[1:]:
@@ -634,6 +634,7 @@
         take_squares(h)
         send_keyvals(1, h)
     take_weight(1, 1, 0)
+    begin(2, 1)
     for h in halves:
         pass_keyvals(1, h)
     for phase in phases[1:]:
@@ -722,7 +723,7 @@
     ctx_count = lax.axis_size("ctx")
     pipe_count = lax.axis_size("pipe")
     state = run_layers(
-        layer_order,
+        layer_order.reshape(1, TICKS),
         activations[0, 0],
         norm_gain[0],
         w_query[0],

time: 126 us -> 117 us (0.929)
  Pallas kernels: 122 us -> 113 us
  local copies, waits for them, and re-layouts: 4.41 us -> 3.11 us
    pallas_call x1, Pallas kernels: 122 us -> 113 us  [run_layers(): pl.pallas_call(functools.partial(layers_kernel, grid), out_shape=jax.Shap...]
    unnamed x2 -> x1, local copies, waits for them, and re-layouts: 4.41 us -> 3.11 us
where the time goes in v2:
time: 117 us; the launch traced here: 116 us
  Pallas kernels  113 us (97%)
  local copies, waits for them, and re-layouts  3.11 us (3%)
    pallas_call x1, Pallas kernels, run_layers(): pl.pallas_call(functools.partial(layers_kernel, grid), out_shape=jax.Shap...  113 us
    unnamed x1, local copies, waits for them, and re-layouts  3.11 us

profile of v2, /device:TPU:0, one launch (start us, length us, event | category | flops | bytes accessed | tf_op | source)
XLA Modules:
  0.0 116.3 jit_solution(3789458522761845961)
XLA Ops:
  0.0 113.1 %shard_map.73 = f32[128,4096]{1,0:T(8,128)} custom-call(s32[1,2]{1,0:T(1,128)} %bitcast.13, f32[128,4096]{1,0:T(8,128)} %bitcast.8, bf16[8,256]{1,0:T(8,128)(2,1)} %bitcast.12, bf16[8,256,512]{2,1,0:T(8,128)(2,1)} %bitcast.9, bf16[8,256,256]{2,1,0:T(8,128)(2,1)} %bitcast.11, bf16[8,512,256]{2,1,0:T(8,128)(2,1)} %bitcast.10, s32[1,2048]{1,0:T(1,128)} %refs_6_.1), custom_call_target="tpu_custom_call" | custom-call | tf_op jit(solution)/shard_map/pallas_call | solution.py:710
  113.1 3.1 %copy.9 = f32[1,1,128,4096]{3,2,1,0:T(8,128)} copy(f32[1,1,128,4096]{3,2,1,0:T(8,128)} %bitcast.7) | data formatting | bytes 4194304

commit v3 on v2

--- a/solution.py
+++ b/solution.py
@@ -37,6 +37,7 @@
             self.along(d, by) for d in self.share_dims for by in range(1, self.sizes[d])
         ]
         self.zero = (0,) * self.rank
+        self.relayed = self.sizes[:2] == (2, 2)
 
     def deltas(self, dims):
         ranges = [range(self.sizes[d]) if d in dims else range(1) for d in range(self.rank)]
@@ -80,6 +81,9 @@
         later_keyval,
         later_query,
         later_out,
+        relay_keyval,
+        relay_query,
+        relay_out,
         part_keyval,
         part_query,
         came_keyval,
@@ -96,6 +100,8 @@
         x_recv,
         w_send,
         w_recv,
+        r_send,
+        r_recv,
         pk_send,
         pk_recv,
         pq_send,
@@ -196,7 +202,7 @@
         )
         greeted += 1
     for by in sorted({1, pipe_count - 1}):
-        for delta in [grid.zero] + grid.hops:
+        for delta in sorted(set([grid.zero] + grid.hops + grid.major)):
             pl.semaphore_signal(
                 barrier,
                 inc=1,
@@ -277,33 +283,51 @@
         used[kind, tick] = count + 1
         return w_send.at[kind, tick, count]
 
+    line = coords[0] * 2 + coords[1] if grid.relayed else 0
+    middle = (line + 1) // 2 == 1 if grid.relayed else False
+    relays = [relay_keyval, relay_query, relay_out]
+
+    def on_line(where):
+        return me + (where - line) * grid.strides[1]
+
     def begin(kind, tick):
         slot = share_slot(grid.zero)
         landing = wholes[kind].at[tick, slot]
         source = landing if tick == 0 else laters[kind]
         pipe = None if tick == 0 else (section + pipe_count - tick) % pipe_count
-        for delta in grid.hops:
+        for delta in grid.hops + [grid.zero] * (tick > 0):
             seen = grid.share.index(grid.minus(grid.zero, delta))
+            recv = w_recv.at[kind, tick, seen]
+            target, where = landing, place(delta)
+            if grid.relayed and delta[0]:
+                recv = r_recv.at[kind, tick, coords[0]]
+                target, where = relays[kind].at[tick, coords[0]], on_line(1 + line % 2)
+            push(remote(source, target, next_send(kind, tick), recv, where, pipe))
+
+    def relay_weight(kind, tick):
+        if not grid.relayed:
+            return
+        for origin in range(2):
+            landing = relays[kind].at[tick, origin]
+            arrival = remote(
+                landing,
+                landing,
+                r_send.at[kind, tick, origin],
+                r_recv.at[kind, tick, origin],
+                on_line(line - 1 + 2 * (1 - origin)),
+            )
+            pl.when(middle)(arrival.wait_recv)
+            seen = grid.share.index(grid.along(0, 1))
+            slot = origin * sizes[2] + coords[2]
             push(
                 remote(
-                    source,
                     landing,
-                    next_send(kind, tick),
+                    wholes[kind].at[tick, slot],
+                    r_send.at[kind, tick, origin],
                     w_recv.at[kind, tick, seen],
-                    place(delta),
-                    pipe,
-                )
-            )
-        if tick:
-            push(
-                remote(
-                    source,
-                    landing,
-                    next_send(kind, tick),
-                    w_recv.at[kind, tick, 0],
-                    me,
-                    pipe,
-                )
+                    on_line(line - 1 + 2 * (1 - origin)),
+                ),
+                middle,
             )
 
     def take_weight(kind, tick, phase):
@@ -454,7 +478,7 @@
                 relay(tick, h, grid.zero, delta, after(h, delta))
         for hop in grid.minor:
             if hop != grid.zero:
-                relay(tick, h, grid.zero, hop, None)
+                relay(tick, h, grid.zero, hop, rank_of(h, hop) > rank_of(h, grid.zero))
 
     def wait_keyvals(tick, h, delta):
         landing = keyvals.at[tick, h, rank_of(h, delta)]
@@ -478,7 +502,8 @@
     def take_keyvals(tick, h):
         for hop in grid.minor:
             if hop != grid.zero:
-                wait_keyvals(tick, h, hop)
+                when = rank_of(h, hop) < rank_of(h, grid.zero)
+                pl.when(when)(functools.partial(wait_keyvals, tick, h, hop))
         for delta in grid.major:
             if delta != grid.zero:
 
@@ -583,8 +608,7 @@
                 ).wait_recv()
             for share in grid.share:
                 cols = columns(place(grid.plus(delta, share)))
-                value = source[:, columns(share_slot(share))].astype(FULL)
-                result[rows(h), cols] = stream[rows(h), cols] + value
+                result[rows(h), cols] = source[:, columns(share_slot(share))]
 
     halves = range(HALVES)
     send_stream(0)
@@ -596,54 +620,60 @@
     load_query.wait()
     load_out.wait()
     fill(1, 0)
+    begin(1, 0)
     fill(2, 0)
+    relay_weight(0, 0)
     for kind in range(3):
         fill(kind, 1)
     for phase in phases:
         take_weight(0, 0, phase)
     take_stream(0)
-    begin(1, 0)
     project(0, 0, 0)
     take_stream(1)
     project(0, 0, 1)
+    begin(2, 0)
+    relay_weight(1, 0)
     for h in halves:
         send_keyvals(0, h)
     take_weight(1, 0, 0)
-    begin(2, 0)
     for h in halves:
         pass_keyvals(0, h)
+    begin(0, 1)
+    relay_weight(2, 0)
     for phase in phases[1:]:
         take_weight(1, 0, phase)
     for h in halves:
         project(1, 0, h)
-    begin(0, 1)
+    begin(1, 1)
+    relay_weight(0, 1)
     take_weight(2, 0, 0)
-    begin(1, 1)
-    for h in halves:
-        attend(0, h)
+    attend(0, 0)
+    attend(0, 1)
+    relay_weight(1, 1)
+    take_weight(0, 1, 0)
     for phase in phases[1:]:
         take_weight(2, 0, phase)
-    take_weight(0, 1, 0)
     mix_first(0)
     for phase in phases[1:]:
         take_weight(0, 1, phase)
     project(0, 1, 0)
     mix_first(1)
     project(0, 1, 1)
+    begin(2, 1)
+    take_weight(1, 1, 0)
     for h in halves:
         take_squares(h)
         send_keyvals(1, h)
-    take_weight(1, 1, 0)
-    begin(2, 1)
+    relay_weight(2, 1)
     for h in halves:
         pass_keyvals(1, h)
+    take_weight(2, 1, 0)
     for phase in phases[1:]:
         take_weight(1, 1, phase)
     for h in halves:
         project(1, 1, h)
-    take_weight(2, 1, 0)
-    for h in halves:
-        attend(1, h)
+    attend(1, 0)
+    attend(1, 1)
     for phase in phases[1:]:
         take_weight(2, 1, phase)
     for h in halves:
@@ -685,6 +715,9 @@
         pltpu.VMEM((block, kv_width), LOW),
         pltpu.VMEM((block, query_width), LOW),
         pltpu.VMEM((query_width, block), LOW),
+        pltpu.VMEM((TICKS, 2, block, kv_width), LOW),
+        pltpu.VMEM((TICKS, 2, block, query_width), LOW),
+        pltpu.VMEM((TICKS, 2, query_width, block), LOW),
         pltpu.VMEM((TICKS, HALVES, split, half, kv_width), LOW),
         pltpu.VMEM((TICKS, HALVES, split, half, query_width), LOW),
         pltpu.VMEM((TICKS, HALVES, split, half, kv_width), LOW),
@@ -701,6 +734,8 @@
         dma((HALVES, split)),
         dma((3, TICKS, share + 2)),
         dma((3, TICKS, share)),
+        dma((3, TICKS, 2)),
+        dma((3, TICKS, 2)),
     ]
     scratch += [dma((TICKS, HALVES, split))] * 4
     scratch += [dma((HALVES, split))] * 2
@@ -709,7 +744,7 @@
     scratch += [dma((HALVES, split))] * 2
     return pl.pallas_call(
         functools.partial(layers_kernel, grid),
-        out_shape=jax.ShapeDtypeStruct(stream.shape, FULL),
+        out_shape=jax.ShapeDtypeStruct(stream.shape, LOW),
         in_specs=[smem] + [hbm] * 5 + [vmem],
         out_specs=vmem,
         scratch_shapes=scratch,
@@ -722,7 +757,7 @@
 def body(activations, norm_gain, w_query, w_keyval, w_out, segment_ids, layer_order):
     ctx_count = lax.axis_size("ctx")
     pipe_count = lax.axis_size("pipe")
-    state = run_layers(
+    change = run_layers(
         layer_order.reshape(1, TICKS),
         activations[0, 0],
         norm_gain[0],
@@ -732,6 +767,7 @@
         segment_ids,
         ctx_count,
     )
+    state = activations[0, 0] + change.astype(FULL)
     if TICKS % pipe_count:
         pairs = [(i, (i + TICKS) % pipe_count) for i in range(pipe_count)]
         state = lax.ppermute(state, "pipe", pairs)

time: 117 us -> 114 us (0.974)
  local copies, waits for them, and re-layouts: 3.11 us -> 0.01 us
  other arithmetic: 0 us -> 2.76 us
  Pallas kernels: 113 us -> 111 us
    unnamed x1 -> x2, local copies, waits for them, and re-layouts: 3.11 us -> 0.01 us
    broadcast_in_dim x0 -> x1, other arithmetic: none -> 2.76 us  [body(): return state[None, None]]
    pallas_call x1, Pallas kernels: 113 us -> 111 us  [run_layers(): pl.pallas_call(functools.partial(layers_kernel, grid), out_shape=jax.Shap...]
where the time goes in v3:
time: 114 us
  Pallas kernels  111 us (97%)
  other arithmetic  2.76 us (2%)
    pallas_call x1, Pallas kernels, run_layers(): pl.pallas_call(functools.partial(layers_kernel, grid), out_shape=jax.Shap...  111 us
    broadcast_in_dim x1, other arithmetic, body(): return state[None, None]  2.76 us

profile of v3, /device:TPU:0, one launch (start us, length us, event | category | flops | bytes accessed | tf_op | source)
XLA Modules:
  0.0 113.8 jit_solution(7481038769614301086)
XLA Ops:
  0.0 0.0 copy-start
  0.0 111.1 %shard_map.73 = bf16[128,4096]{1,0:T(8,128)(2,1)} custom-call(s32[1,2]{1,0:T(1,128)} %bitcast.14, f32[128,4096]{1,0:T(8,128)} %bitcast.9, bf16[8,256]{1,0:T(8,128)(2,1)} %bitcast.13, bf16[8,256,512]{2,1,0:T(8,128)(2,1)} %bitcast.10, bf16[8,256,256]{2,1,0:T(8,128)(2,1)} %bitcast.12, bf16[8,512,256]{2,1,0:T(8,128)(2,1)} %bitcast.11, s32[1,2048]{1,0:T(1,128)} %refs_6_.1), custom_call_target="tpu_custom_call" | custom-call | tf_op jit(solution)/shard_map/pallas_call | solution.py:745
  111.1 0.0 copy-done
  111.1 2.8 %add_bitcast_fusion = f32[1,1,128,4096]{3,2,1,0:T(8,128)} fusion(bf16[128,4096]{1,0:T(8,128)(2,1)} %shard_map.73, f32[1,1,128,4096]{3,2,1,0:T(8,128)S(1)} %copy-done), kind=kLoop, calls=%fused_computation | loop fusion | flops 1048576 | bytes 5242880 | tf_op jit(solution)/shard_map/broadcast_in_dim | solution.py:774
Async XLA Ops:
  0.0 111.1 %copy-start = (f32[1,1,128,4096]{3,2,1,0:T(8,128)S(1)}, f32[1,1,128,4096]{3,2,1,0:T(8,128)}, u32[]{:S(2)}) copy-start(f32[1,1,128,4096]{3,2,1,0:T(8,128)} %param.7) | copy-start | bytes 6291460

commit v4 on v3

--- a/solution.py
+++ b/solution.py
@@ -183,10 +183,10 @@
         loads.append(copy)
         return copy
 
-    load_stream = [load(stream_hbm.at[rows(h)], stream.at[rows(h)]) for h in range(HALVES)]
     load_gain = load(gain_hbm, gains)
     load_keyval = load(keyval_hbm, keyval_all)
     load_query = load(query_hbm, query_all)
+    load_stream = [load(stream_hbm.at[rows(h)], stream.at[rows(h)]) for h in range(HALVES)]
     load_out = load(out_hbm, out_all)
 
     keyvals[...] = jnp.zeros_like(keyvals)
@@ -220,21 +220,21 @@
         own = jnp.sum(jnp.where(key_rel == query_rel, seg, 0.0), axis=1, keepdims=True)
         bias[h] = jnp.where((key_rel <= query_rel) & (seg == own), 0.0, -1e30)
 
-    pl.semaphore_wait(barrier, greeted)
-
-    others = [delta for delta in grid.split if delta != grid.zero]
     factors = {}
 
-    def send_stream(h):
+    def cast_stream(h):
         load_stream[h].wait()
         squares = jnp.zeros((half, 1), FULL)
         for index, delta in enumerate(grid.split):
             target = kept.at[h, split_slot(grid.zero)] if delta == grid.zero else sent.at[h, index]
-            for s, share in enumerate(grid.share):
-                where = grid.plus(delta, share)
-                value = stream[rows(h), columns(place(where))]
+            for share in grid.share:
+                value = stream[rows(h), columns(place(grid.plus(delta, share)))]
                 squares += jnp.sum(value * value, axis=1, keepdims=True)
                 target[:, columns(share_slot(share))] = value.astype(LOW)
+        factors[0, h] = lax.rsqrt(squares / model_width + 1e-05)
+
+    def send_stream(h):
+        for index, delta in enumerate(grid.split):
             if delta != grid.zero:
                 seen = grid.split.index(grid.minus(grid.zero, delta))
                 push(
@@ -246,7 +246,6 @@
                         place(delta),
                     )
                 )
-        factors[0, h] = lax.rsqrt(squares / model_width + 1e-05)
 
     def take_stream(h):
         for index, delta in enumerate(grid.split):
@@ -611,31 +610,34 @@
                 result[rows(h), cols] = source[:, columns(share_slot(share))]
 
     halves = range(HALVES)
-    send_stream(0)
     load_gain.wait()
     load_keyval.wait()
     fill(0, 0)
+    load_query.wait()
+    fill(1, 0)
+    cast_stream(0)
+    pl.semaphore_wait(barrier, greeted)
     begin(0, 0)
+    begin(1, 0)
+    send_stream(0)
+    cast_stream(1)
     send_stream(1)
-    load_query.wait()
     load_out.wait()
-    fill(1, 0)
-    begin(1, 0)
     fill(2, 0)
     relay_weight(0, 0)
     for kind in range(3):
         fill(kind, 1)
     for phase in phases:
         take_weight(0, 0, phase)
+    relay_weight(1, 0)
     take_stream(0)
     project(0, 0, 0)
+    take_weight(1, 0, 0)
     take_stream(1)
     project(0, 0, 1)
     begin(2, 0)
-    relay_weight(1, 0)
     for h in halves:
         send_keyvals(0, h)
-    take_weight(1, 0, 0)
     for h in halves:
         pass_keyvals(0, h)
     begin(0, 1)

time: 114 us -> 113 us (level)
    pallas_call x1, Pallas kernels: 111 us -> 110 us  [run_layers(): pl.pallas_call(functools.partial(layers_kernel, grid), out_shape=jax.Shap...]
where the time goes in v4:
time: 113 us; the launch traced here: 112 us
  Pallas kernels  110 us (97%)
  other arithmetic  2.76 us (2%)
    pallas_call x1, Pallas kernels, run_layers(): pl.pallas_call(functools.partial(layers_kernel, grid), out_shape=jax.Shap...  110 us
    broadcast_in_dim x1, other arithmetic, body(): return state[None, None]  2.76 us

profile of v4, /device:TPU:0, one launch (start us, length us, event | category | flops | bytes accessed | tf_op | source)
XLA Modules:
  0.0 112.4 jit_solution(18003435958245332721)
XLA Ops:
  0.0 0.0 copy-start
  0.0 109.6 %shard_map.73 = bf16[128,4096]{1,0:T(8,128)(2,1)} custom-call(s32[1,2]{1,0:T(1,128)} %bitcast.14, f32[128,4096]{1,0:T(8,128)} %bitcast.9, bf16[8,256]{1,0:T(8,128)(2,1)} %bitcast.13, bf16[8,256,512]{2,1,0:T(8,128)(2,1)} %bitcast.10, bf16[8,256,256]{2,1,0:T(8,128)(2,1)} %bitcast.12, bf16[8,512,256]{2,1,0:T(8,128)(2,1)} %bitcast.11, s32[1,2048]{1,0:T(1,128)} %refs_6_.1), custom_call_target="tpu_custom_call" | custom-call | tf_op jit(solution)/shard_map/pallas_call | solution.py:747
  109.6 0.0 copy-done
  109.6 2.8 %add_bitcast_fusion = f32[1,1,128,4096]{3,2,1,0:T(8,128)} fusion(bf16[128,4096]{1,0:T(8,128)(2,1)} %shard_map.73, f32[1,1,128,4096]{3,2,1,0:T(8,128)S(1)} %copy-done), kind=kLoop, calls=%fused_computation | loop fusion | flops 1048576 | bytes 5242880 | tf_op jit(solution)/shard_map/broadcast_in_dim | solution.py:776
Async XLA Ops:
  0.0 109.6 %copy-start = (f32[1,1,128,4096]{3,2,1,0:T(8,128)S(1)}, f32[1,1,128,4096]{3,2,1,0:T(8,128)}, u32[]{:S(2)}) copy-start(f32[1,1,128,4096]{3,2,1,0:T(8,128)} %param.7) | copy-start | bytes 6291460
